TPU v7x, 128 devices: a whole 4x4x4 slice. The times are simulated.
128 devices in a mesh: expert: 8 (over z_lo, y), dp: 16 (over z_hi, x, core).
Axes of the slice: x: 4, y: 4, z: 4 (z_hi: 2, z_lo: 2; z = z_hi * 2 + z_lo), core: 2. Of those that a mesh axis runs over, the one named last changes fastest.
Arguments:
- tokens: bfloat16 [2048, 7168], P('dp', 'expert'), may hold values from -6 to 6
- grad_out: bfloat16 [2048, 7168], P('dp', 'expert'), may hold values from -6 to 6
- expert_ids: int32 [2048, 2], P('dp'), may hold values from -1 to 7, as said below
- route_weights: float32 [2048, 2], P('dp'), may hold values from 0.1 to 1
- w_gate: bfloat16 [8, 7168, 2048], P('expert', 'dp'), may hold values from -0.0625 to 0.0625
- w_up: bfloat16 [8, 7168, 2048], P('expert', 'dp'), may hold values from -0.0625 to 0.0625
- w_down: bfloat16 [8, 2048, 7168], P('expert', None, 'dp'), may hold values from -0.125 to 0.125
Outputs:
- grad_tokens: bfloat16 [2048, 7168], P('dp', 'expert')
- grad_gate: bfloat16 [8, 7168, 2048], P('expert', 'dp')
- grad_up: bfloat16 [8, 7168, 2048], P('expert', 'dp')
- grad_down: bfloat16 [8, 2048, 7168], P('expert', None, 'dp')
Inputs may be any that keep to these rules, and one draw needn't show every extreme that they name: expert_ids[t, 0] is an expert; expert_ids[t, 1] is another expert or -1. Within each block of 128 rows (the tokens of one index of dp) no expert appears in more than 64 rows, and one expert, the same in every block, appears in exactly 64 rows, each of which has -1 as its second entry.
All inputs are finite; a program needn't handle non-finite values.
Results may differ from a plain program's by a relative error of at most 0.03.
Values may be sent and summed in bfloat16 or wider, within the bound.
A program may use at most 128 MiB of HBM per device.

v0:
```python
import math
import jax
import jax.numpy as jnp
from jax import lax
from jax.sharding import PartitionSpec as P


def body(tokens, grad_out, expert_ids, route_weights, w_gate, w_up, w_down):
    experts = lax.axis_size("expert")
    groups = lax.axis_size("dp")
    tok_rows = tokens.shape[0]
    capacity = tok_rows // 2
    hidden = w_gate.shape[2]
    slots = groups * capacity
    expert_index = lax.axis_index("expert")
    inv_root = 1.0 / math.sqrt(tok_rows * groups)
    rows_first = (((0,), (0,)), ((), ()))
    last_dims = (((1,), (1,)), ((), ()))
    routed = expert_ids >= 0
    matches = (
        expert_ids[:, :, None] == jnp.arange(experts, dtype=jnp.int32)[None, None, :]
    ).astype(jnp.int32)
    flat_match = matches.reshape(tok_rows * 2, experts)
    position = jnp.sum(flat_match * (jnp.cumsum(flat_match, axis=0) - 1), axis=1).reshape(
        tok_rows, 2
    )
    slot_ids = jnp.where(routed, expert_ids * capacity + position, -1)
    slot_match = (
        slot_ids[None, :, :] == jnp.arange(experts * capacity, dtype=jnp.int32)[:, None, None]
    ).astype(jnp.float32)
    dispatch = jnp.sum(slot_match, axis=2).astype(jnp.bfloat16)
    slot_weight = jnp.einsum("stk,tk->s", slot_match, route_weights)
    own_weight = lax.dynamic_slice_in_dim(slot_weight, expert_index * capacity, capacity)
    send_x = (
        jnp.dot(dispatch, tokens, preferred_element_type=jnp.float32)
        .astype(jnp.bfloat16)
        .reshape(experts, capacity, -1)
    )
    send_g = (
        jnp.dot(dispatch, grad_out, preferred_element_type=jnp.float32)
        .astype(jnp.bfloat16)
        .reshape(experts, capacity, -1)
    )
    recv_x, recv_g = (
        lax.all_to_all(
            lax.all_to_all(send_x, "expert", split_axis=0, concat_axis=2, tiled=True),
            "dp",
            split_axis=2,
            concat_axis=1,
            tiled=True,
        ),
        lax.all_to_all(
            lax.all_to_all(send_g, "expert", split_axis=0, concat_axis=2, tiled=True),
            "dp",
            split_axis=2,
            concat_axis=1,
            tiled=True,
        ),
    )
    feature_rows = recv_x.reshape(slots, -1)
    grad_rows = recv_g.reshape(slots, -1)
    gate_shard = w_gate[0]
    up_shard = w_up[0]
    down_shard = w_down[0]
    shard_width = gate_shard.shape[0]
    x_block = feature_rows
    g_block = grad_rows
    gate = jnp.dot(x_block, gate_shard, preferred_element_type=jnp.float32)
    upper = jnp.dot(x_block, up_shard, preferred_element_type=jnp.float32)
    back = lax.dot_general(g_block, down_shard, last_dims, preferred_element_type=jnp.float32)
    mine = lax.psum_scatter(
        jnp.concatenate([gate, upper, back], axis=1).astype(jnp.bfloat16),
        "dp",
        scatter_dimension=0,
        tiled=True,
    ).astype(jnp.float32)
    gate = mine[:, :hidden]
    upper = mine[:, hidden : 2 * hidden]
    back = mine[:, 2 * hidden :] * own_weight[:, None]
    sigmoid_gate = jax.nn.sigmoid(gate)
    scaled = own_weight[:, None] * gate * sigmoid_gate * upper
    d_gate = back * upper * sigmoid_gate * (1.0 + gate * (1.0 - sigmoid_gate))
    d_up = back * gate * sigmoid_gate
    local = jnp.concatenate([scaled, d_gate, d_up], axis=1).astype(jnp.bfloat16)
    piece = lax.all_gather(local, "dp", axis=0, tiled=True)
    x_block = feature_rows
    g_block = grad_rows
    scaled = piece[:, :hidden]
    d_gate = piece[:, hidden : 2 * hidden]
    d_up = piece[:, 2 * hidden :]
    grad_g = lax.dot_general(x_block, d_gate, rows_first, preferred_element_type=jnp.float32)
    grad_u = lax.dot_general(x_block, d_up, rows_first, preferred_element_type=jnp.float32)
    grad_d = lax.dot_general(scaled, g_block, rows_first, preferred_element_type=jnp.float32)
    block_dx = lax.dot_general(
        d_gate, gate_shard, last_dims, preferred_element_type=jnp.float32
    ) + lax.dot_general(d_up, up_shard, last_dims, preferred_element_type=jnp.float32)
    dx_rows = block_dx.astype(jnp.bfloat16)
    grad_g, grad_u, grad_d, dx_rows = (grad_g, grad_u, grad_d, dx_rows)
    returned = lax.all_to_all(
        lax.all_to_all(
            dx_rows.reshape(1, slots, shard_width), "dp", split_axis=1, concat_axis=2, tiled=True
        ),
        "expert",
        split_axis=2,
        concat_axis=0,
        tiled=True,
    )
    returned = returned.reshape(experts * capacity, -1)
    grad_tokens = lax.dot_general(
        dispatch, returned, rows_first, preferred_element_type=jnp.float32
    ).astype(jnp.bfloat16)
    grad_gate = (grad_g * inv_root).astype(jnp.bfloat16)[None]
    grad_up = (grad_u * inv_root).astype(jnp.bfloat16)[None]
    grad_down = (grad_d * inv_root).astype(jnp.bfloat16)[None]
    return (grad_tokens, grad_gate, grad_up, grad_down)


def solution(mesh):
    in_specs = (
        P("dp", "expert"),
        P("dp", "expert"),
        P("dp", None),
        P("dp", None),
        P("expert", "dp", None),
        P("expert", "dp", None),
        P("expert", None, "dp"),
    )
    out_specs = (
        P("dp", "expert"),
        P("expert", "dp", None),
        P("expert", "dp", None),
        P("expert", None, "dp"),
    )
    return jax.shard_map(body, mesh=mesh, in_specs=in_specs, out_specs=out_specs, check_vma=False)
```

profile of v0, /device:TPU:1, one launch (start us, length us, event | category | flops | bytes accessed | tf_op | source)
XLA Modules:
  0.0 595.4 jit_solution(15682744833489243268)
XLA Ops:
  12.6 6.4 %all-to-all-start.2 = ((bf16[8,64,896]{2,1,0:T(8,128)(2,1)}), bf16[8,64,896]{2,1,0:T(8,128)(2,1)S(1)}, u32[]{:S(2)}, u32[]{:S(2)}) async-start(bf16[8,64,896]{2,1,0:T(8,128)(2,1)} %bitcast.12), calls=%async_computation.2 | async-start | bytes 1835008 | tf_op jit(solution)/shard_map/all_to_all | solution.py:53
  20.3 13.1 %all-to-all-done.2 = bf16[8,64,896]{2,1,0:T(8,128)(2,1)S(1)} async-done(((bf16[8,64,896]{2,1,0:T(8,128)(2,1)}), bf16[8,64,896]{2,1,0:T(8,128)(2,1)S(1)}, u32[]{:S(2)}, u32[]{:S(2)}) %all-to-all-start.2) | async-done | bytes 917536 | tf_op jit(solution)/shard_map/all_to_all | solution.py:53
  40.4 11.1 %reshape.65 = bf16[1,64,7168]{1,0,2:T(2,128)(2,1)} reshape(bf16[1,64,8,896]{1,3,2,0:T(8,128)(2,1)} %copy.97) | data formatting | bytes 1835008 | tf_op jit(solution)/shard_map/all_to_all | solution.py:53
  52.1 41.0 %reduce.2 = bf16[7168,64]{1,0:T(8,128)(2,1)} reduce(bf16[7168,1,64]{2,1,0:T(2,128)(2,1)} %bitcast.92, bf16[]{:T(256)} %broadcast.46), dimensions={1}, to_apply=%bitcast.70.reduce_sub_computation | reduce | bytes 1835010
  93.1 4.3 reshape.68
  97.3 8.5 %all-to-all-start.3 = ((bf16[16,2,14336]{2,1,0:T(2,128)(2,1)}), bf16[16,2,14336]{2,1,0:T(2,128)(2,1)}, u32[]{:S(2)}, u32[]{:S(2)}) async-start(bf16[16,2,14336]{2,1,0:T(2,128)(2,1)} %reshape.68), calls=%async_computation.3 | async-start | bytes 1835008 | tf_op jit(solution)/shard_map/all_to_all | solution.py:52
  107.5 11.1 %reshape.64 = bf16[1,64,7168]{1,0,2:T(2,128)(2,1)} reshape(bf16[1,64,8,896]{1,3,2,0:T(8,128)(2,1)} %copy.96) | data formatting | bytes 1835008 | tf_op jit(solution)/shard_map/all_to_all | solution.py:46
  118.7 41.0 %reduce.3 = bf16[7168,64]{1,0:T(8,128)(2,1)} reduce(bf16[7168,1,64]{2,1,0:T(2,128)(2,1)} %bitcast.94, bf16[]{:T(256)} %broadcast.46), dimensions={1}, to_apply=%bitcast.72.reduce_sub_computation | reduce | bytes 1835010
  159.7 4.3 reshape.70
  163.9 7.2 %all-to-all-start.1 = ((bf16[16,2,14336]{2,1,0:T(2,128)(2,1)}), bf16[16,2,14336]{2,1,0:T(2,128)(2,1)}, u32[]{:S(2)}, u32[]{:S(2)}) async-start(bf16[16,2,14336]{2,1,0:T(2,128)(2,1)} %reshape.70), calls=%async_computation.1 | async-start | bytes 1835008 | tf_op jit(solution)/shard_map/all_to_all | solution.py:45
  171.6 9.9 %reshape.69 = bf16[7168,1,64]{2,1,0:T(2,128)(2,1)} reshape(bf16[16,2,14336]{2,1,0:T(2,128)(2,1)} %all-to-all-done.3) | data formatting | bytes 1835008
  181.5 8.1 %copy.88 = bf16[1,64,7168]{2,1,0:T(8,128)(2,1)} copy(bf16[1,64,7168]{1,0,2:T(2,128)(2,1)} %bitcast.95) | data formatting | bytes 1835008 | tf_op jit(solution)/shard_map/all_to_all | solution.py:52
  193.6 9.9 %reshape.71 = bf16[7168,1,64]{2,1,0:T(2,128)(2,1)} reshape(bf16[16,2,14336]{2,1,0:T(2,128)(2,1)} %all-to-all-done.1) | data formatting | bytes 1835008
  203.5 8.1 %copy.84 = bf16[1,64,7168]{2,1,0:T(8,128)(2,1)} copy(bf16[1,64,7168]{1,0,2:T(2,128)(2,1)} %bitcast.96) | data formatting | bytes 1835008 | tf_op jit(solution)/shard_map/all_to_all | solution.py:45
  221.7 11.3 %pad_maximum_fusion = bf16[1024,6144]{1,0:T(8,128)(2,1)} fusion(bf16[1024,2048]{1,0:T(8,128)(2,1)S(1)} %convolution_convert_fusion, bf16[1024,2048]{1,0:T(8,128)(2,1)S(1)} %convolution_convert_fusion.1, bf16[1024,2048]{1,0:T(8,128)(2,1)S(1)} %convolution_convert_fusion.2), kind=kLoop, calls=%fused_computation | loop fusion | flops 37748736 | bytes 25165824 | tf_op jit(solution)/shard_map/concatenate | solution.py:72
  234.0 122.2 %reduce-scatter.2.cloned.1.call-done = bf16[64,6144]{1,0:T(8,128)(2,1)} async-done(((bf16[1024,6144]{1,0:T(8,128)(2,1)}), bf16[64,6144]{1,0:T(8,128)(2,1)}) %reduce-scatter.2.cloned.1.call-update) | async-done | bytes 786448 | tf_op jit(solution)/shard_map/reduce_scatter | solution.py:71
  358.8 91.2 %all-gather.2.cloned.1.call-done = bf16[1024,6144]{1,0:T(8,128)(2,1)} async-done(((bf16[64,6144]{1,0:T(8,128)(2,1)}), bf16[1024,6144]{1,0:T(8,128)(2,1)}) %all-gather.2.cloned.1.call-update) | async-done | bytes 12582928 | tf_op jit(solution)/shard_map/all_gather | solution.py:85
  449.9 4.4 fusion.4
  454.3 4.4 fusion.34
  458.7 3.9 copy.90
  462.6 8.3 %reduce.4 = bf16[1024,448]{1,0:T(8,128)(2,1)S(1)} reduce(bf16[1024,1,448]{2,1,0:T(2,128)(2,1)} %bitcast.98, bf16[]{:T(256)} %broadcast.46), dimensions={1}, to_apply=%bitcast.74.reduce_sub_computation | reduce | bytes 1835010
  473.0 3.9 all-to-all-start.4
  476.9 5.8 fusion.16
  482.7 10.2 %all-to-all-done.4 = bf16[16,2,14336]{2,1,0:T(2,128)(2,1)S(1)} async-done(((bf16[16,2,14336]{2,1,0:T(2,128)(2,1)}), bf16[16,2,14336]{2,1,0:T(2,128)(2,1)S(1)}, u32[]{:S(2)}, u32[]{:S(2)}) %all-to-all-start.4) | async-done | bytes 917536 | tf_op jit(solution)/shard_map/all_to_all | solution.py:100
  500.2 11.1 %reshape.66 = bf16[1,64,7168]{1,0,2:T(2,128)(2,1)} reshape(bf16[1,64,16,448]{1,3,2,0:T(8,128)(2,1)} %copy.98) | data formatting | bytes 1835008 | tf_op jit(solution)/shard_map/all_to_all | solution.py:100
  511.3 41.0 %reduce.5 = bf16[7168,64]{1,0:T(8,128)(2,1)} reduce(bf16[7168,1,64]{2,1,0:T(2,128)(2,1)} %bitcast.93, bf16[]{:T(256)} %broadcast.46), dimensions={1}, to_apply=%bitcast.76.reduce_sub_computation | reduce | bytes 1835010
  552.3 4.3 reshape.74
  556.6 4.4 all-to-all-start.5
  561.0 5.9 fusion.19
  566.9 5.5 fusion.22
  575.4 4.1 reshape.75
  579.5 7.2 %copy.93 = bf16[1,64,7168]{2,1,0:T(8,128)(2,1)S(1)} copy(bf16[1,64,7168]{1,0,2:T(2,128)(2,1)} %bitcast.97) | data formatting | bytes 1835008 | tf_op jit(solution)/shard_map/all_to_all | solution.py:99
  (67 shorter events, 47.4 us)
Async XLA Ops:
  7.2 207.4 %copy-start = (bf16[1,448,2048]{2,1,0:T(8,128)(2,1)S(1)}, bf16[1,448,2048]{2,1,0:T(8,128)(2,1)}, u32[]{:S(2)}) copy-start(bf16[1,448,2048]{2,1,0:T(8,128)(2,1)} %param.12) | copy-start | bytes 5505028
  7.2 11.8 %copy-start.5 = (bf16[128,896]{1,0:T(8,128)(2,1)S(1)}, bf16[128,896]{1,0:T(8,128)(2,1)}, u32[]{:S(2)}) copy-start(bf16[128,896]{1,0:T(8,128)(2,1)} %param.7) | copy-start | bytes 688132
  12.6 20.8 %all-to-all-start.2 = ((bf16[8,64,896]{2,1,0:T(8,128)(2,1)}), bf16[8,64,896]{2,1,0:T(8,128)(2,1)S(1)}, u32[]{:S(2)}, u32[]{:S(2)}) async-start(bf16[8,64,896]{2,1,0:T(8,128)(2,1)} %bitcast.12), calls=%async_computation.2 | async-start | bytes 1835008 | tf_op jit(solution)/shard_map/all_to_all | solution.py:53
  33.4 0.9 copy-start.1
  34.3 63.0 %all-to-all-start = ((bf16[8,64,896]{2,1,0:T(8,128)(2,1)}), bf16[8,64,896]{2,1,0:T(8,128)(2,1)S(1)}, u32[]{:S(2)}, u32[]{:S(2)}) async-start(bf16[8,64,896]{2,1,0:T(8,128)(2,1)} %bitcast.5), calls=%async_computation | async-start | bytes 1835008 | tf_op jit(solution)/shard_map/all_to_all | solution.py:46
  97.3 66.6 %all-to-all-start.3 = ((bf16[16,2,14336]{2,1,0:T(2,128)(2,1)}), bf16[16,2,14336]{2,1,0:T(2,128)(2,1)}, u32[]{:S(2)}, u32[]{:S(2)}) async-start(bf16[16,2,14336]{2,1,0:T(2,128)(2,1)} %reshape.68), calls=%async_computation.3 | async-start | bytes 1835008 | tf_op jit(solution)/shard_map/all_to_all | solution.py:52
  163.9 29.7 %all-to-all-start.1 = ((bf16[16,2,14336]{2,1,0:T(2,128)(2,1)}), bf16[16,2,14336]{2,1,0:T(2,128)(2,1)}, u32[]{:S(2)}, u32[]{:S(2)}) async-start(bf16[16,2,14336]{2,1,0:T(2,128)(2,1)} %reshape.70), calls=%async_computation.1 | async-start | bytes 1835008 | tf_op jit(solution)/shard_map/all_to_all | solution.py:45
  171.2 185.0 %reduce-scatter.2.cloned.1.call-start = ((), (), s32[]{:S(2)}) async-start(), calls=%async_computation.7 | async-start | bytes 13369344 | tf_op jit(solution)/shard_map/reduce_scatter | solution.py:71
  214.6 2.4 copy-start.4
  214.6 2.4 copy-start.7
  217.0 2.4 copy-start.2
  217.0 2.4 copy-start.6
  233.0 0.7 copy-start.9
  233.0 216.9 %all-gather.2.cloned.1.call-start = ((), (), s32[]{:S(2)}) async-start(), calls=%async_computation.8 | async-start | bytes 13369344 | tf_op jit(solution)/shard_map/all_gather | solution.py:85
  449.9 4.4 copy-start.8
  473.0 19.9 %all-to-all-start.4 = ((bf16[16,2,14336]{2,1,0:T(2,128)(2,1)}), bf16[16,2,14336]{2,1,0:T(2,128)(2,1)S(1)}, u32[]{:S(2)}, u32[]{:S(2)}) async-start(bf16[16,2,14336]{2,1,0:T(2,128)(2,1)} %reshape.72), calls=%async_computation.5 | async-start | bytes 1835008 | tf_op jit(solution)/shard_map/all_to_all | solution.py:100
  556.6 18.8 %all-to-all-start.5 = ((bf16[8,2,28672]{2,1,0:T(2,128)(2,1)}), bf16[8,2,28672]{2,1,0:T(2,128)(2,1)S(1)}, u32[]{:S(2)}, u32[]{:S(2)}) async-start(bf16[8,2,28672]{2,1,0:T(2,128)(2,1)} %reshape.74), calls=%async_computation.6 | async-start | bytes 1835008 | tf_op jit(solution)/shard_map/all_to_all | solution.py:99
  561.0 5.9 copy-start.3
Sparse Core Ops, SparseCore 0:
  233.1 123.0 reduce-scatter.1
  359.5 90.3 all-gather.1
where the time goes:
time: 606 us; the launch traced here: 595 us
  waiting for transfers between devices  240 us (40%)
  other arithmetic  147 us (24%)
  local copies, waits for them, and re-layouts  122 us (20%)
  matrix products  37.9 us (6%)
  starting transfers between devices  34.6 us (6%)
  between operations  14.8 us (2%)
    unnamed x4, other arithmetic  131 us
    reduce_scatter x1, waiting for transfers between devices, body(): lax.psum_scatter(jnp.concatenate([gate, upper, back], axis=1).astype(jnp....  122 us
    all_gather x1, waiting for transfers between devices, body(): piece = lax.all_gather(local, 'dp', axis=0, tiled=True)  91.2 us
    unnamed x32, local copies, waits for them, and re-layouts  47.4 us
    all_to_all x2, local copies, waits for them, and re-layouts, body(): lax.all_to_all(send_g, 'expert', split_axis=0, concat_axis=2, tiled=True)  13.7 us
    all_to_all x1, waiting for transfers between devices, body(): lax.all_to_all(send_g, 'expert', split_axis=0, concat_axis=2, tiled=True)  13.1 us
    all_to_all x2, local copies, waits for them, and re-layouts, body(): lax.all_to_all(dx_rows.reshape(1, slots, shard_width), 'dp', split_axis=1...  12.8 us
    all_to_all x2, local copies, waits for them, and re-layouts, body(): lax.all_to_all(send_x, 'expert', split_axis=0, concat_axis=2, tiled=True)  12.8 us
  transfers between devices with their start and end apart: 8, of which 5 were waited for; matrix products, arithmetic and copies ran while one was open for 26% of the time, Pallas kernels for 0%

commit v1 on v0

--- a/solution.py
+++ b/solution.py
@@ -82,7 +82,9 @@
     d_gate = back * upper * sigmoid_gate * (1.0 + gate * (1.0 - sigmoid_gate))
     d_up = back * gate * sigmoid_gate
     local = jnp.concatenate([scaled, d_gate, d_up], axis=1).astype(jnp.bfloat16)
-    piece = lax.all_gather(local, "dp", axis=0, tiled=True)
+    piece = jnp.concatenate(
+        lax.all_to_all(jnp.stack([local] * lax.axis_size("dp")), "dp", 0, 0), axis=0
+    )
     x_block = feature_rows
     g_block = grad_rows
     scaled = piece[:, :hidden]

time: 606 us -> 666 us (1.099)
  blocking collectives: 0 us -> 146 us
  waiting for transfers between devices: 240 us -> 148 us
  local copies, waits for them, and re-layouts: 122 us -> 131 us
    all_to_all x0 -> x1, blocking collectives: none -> 146 us  [body(): lax.all_to_all(jnp.stack([local] * lax.axis_size('dp')), 'dp', 0, 0)]
    all_gather x1 -> x0, waiting for transfers between devices: 91.2 us -> none  [body(): piece = lax.all_gather(local, 'dp', axis=0, tiled=True)]
    unnamed x32 -> x34, local copies, waits for them, and re-layouts: 47.4 us -> 50.4 us
  transfers between devices with their start and end apart: 8 -> 7, of which waited for: 5 -> 4; matrix products, arithmetic and copies ran while one was open for 26% -> 24% of each run, Pallas kernels for 0% -> 0%
where the time goes in v1:
time: 666 us; the launch traced here: 655 us
  waiting for transfers between devices  148 us (22%)
  other arithmetic  146 us (22%)
  blocking collectives  146 us (22%)
  local copies, waits for them, and re-layouts  131 us (20%)
  starting transfers between devices  35.6 us (5%)
  matrix products  33.3 us (5%)
  between operations  14.8 us (2%)
    all_to_all x1, blocking collectives, body(): lax.all_to_all(jnp.stack([local] * lax.axis_size('dp')), 'dp', 0, 0)  146 us
    unnamed x4, other arithmetic  131 us
    reduce_scatter x1, waiting for transfers between devices, body(): lax.psum_scatter(jnp.concatenate([gate, upper, back], axis=1).astype(jnp....  122 us
    unnamed x34, local copies, waits for them, and re-layouts  50.4 us
    all_to_all x2, local copies, waits for them, and re-layouts, body(): lax.all_to_all(send_g, 'expert', split_axis=0, concat_axis=2, tiled=True)  13.7 us
  transfers between devices with their start and end apart: 7, of which 4 were waited for; matrix products, arithmetic and copies ran while one was open for 24% of the time, Pallas kernels for 0%

profile of v1, /device:TPU:1, one launch (start us, length us, event | category | flops | bytes accessed | tf_op | source)
XLA Modules:
  0.0 654.7 jit_solution(2940743966294731631)
XLA Ops:
  12.6 6.4 all-to-all-start.2
  20.3 13.1 %all-to-all-done.2 = bf16[8,64,896]{2,1,0:T(8,128)(2,1)S(1)} async-done(((bf16[8,64,896]{2,1,0:T(8,128)(2,1)}), bf16[8,64,896]{2,1,0:T(8,128)(2,1)S(1)}, u32[]{:S(2)}, u32[]{:S(2)}) %all-to-all-start.2) | async-done | bytes 917536 | tf_op jit(solution)/shard_map/all_to_all | solution.py:53
  40.4 11.1 %reshape.79 = bf16[1,64,7168]{1,0,2:T(2,128)(2,1)} reshape(bf16[1,64,8,896]{1,3,2,0:T(8,128)(2,1)} %copy.97) | data formatting | bytes 1835008 | tf_op jit(solution)/shard_map/all_to_all | solution.py:53
  52.1 41.0 %reduce.2 = bf16[7168,64]{1,0:T(8,128)(2,1)} reduce(bf16[7168,1,64]{2,1,0:T(2,128)(2,1)} %bitcast.93, bf16[]{:T(256)} %broadcast.47), dimensions={1}, to_apply=%bitcast.71.reduce_sub_computation | reduce | bytes 1835010
  93.1 4.3 reshape.82
  97.3 8.5 %all-to-all-start.3 = ((bf16[16,2,14336]{2,1,0:T(2,128)(2,1)}), bf16[16,2,14336]{2,1,0:T(2,128)(2,1)}, u32[]{:S(2)}, u32[]{:S(2)}) async-start(bf16[16,2,14336]{2,1,0:T(2,128)(2,1)} %reshape.82), calls=%async_computation.3 | async-start | bytes 1835008 | tf_op jit(solution)/shard_map/all_to_all | solution.py:52
  107.5 11.1 %reshape.78 = bf16[1,64,7168]{1,0,2:T(2,128)(2,1)} reshape(bf16[1,64,8,896]{1,3,2,0:T(8,128)(2,1)} %copy.96) | data formatting | bytes 1835008 | tf_op jit(solution)/shard_map/all_to_all | solution.py:46
  118.7 41.0 %reduce.3 = bf16[7168,64]{1,0:T(8,128)(2,1)} reduce(bf16[7168,1,64]{2,1,0:T(2,128)(2,1)} %bitcast.95, bf16[]{:T(256)} %broadcast.47), dimensions={1}, to_apply=%bitcast.73.reduce_sub_computation | reduce | bytes 1835010
  159.7 4.3 reshape.84
  163.9 7.2 %all-to-all-start.1 = ((bf16[16,2,14336]{2,1,0:T(2,128)(2,1)}), bf16[16,2,14336]{2,1,0:T(2,128)(2,1)}, u32[]{:S(2)}, u32[]{:S(2)}) async-start(bf16[16,2,14336]{2,1,0:T(2,128)(2,1)} %reshape.84), calls=%async_computation.1 | async-start | bytes 1835008 | tf_op jit(solution)/shard_map/all_to_all | solution.py:45
  171.6 9.9 %reshape.83 = bf16[7168,1,64]{2,1,0:T(2,128)(2,1)} reshape(bf16[16,2,14336]{2,1,0:T(2,128)(2,1)} %all-to-all-done.3) | data formatting | bytes 1835008
  181.5 8.1 %copy.88 = bf16[1,64,7168]{2,1,0:T(8,128)(2,1)} copy(bf16[1,64,7168]{1,0,2:T(2,128)(2,1)} %bitcast.96) | data formatting | bytes 1835008 | tf_op jit(solution)/shard_map/all_to_all | solution.py:52
  193.6 9.9 %reshape.85 = bf16[7168,1,64]{2,1,0:T(2,128)(2,1)} reshape(bf16[16,2,14336]{2,1,0:T(2,128)(2,1)} %all-to-all-done.1) | data formatting | bytes 1835008
  203.5 8.1 %copy.84 = bf16[1,64,7168]{2,1,0:T(8,128)(2,1)} copy(bf16[1,64,7168]{1,0,2:T(2,128)(2,1)} %bitcast.97) | data formatting | bytes 1835008 | tf_op jit(solution)/shard_map/all_to_all | solution.py:45
  221.7 11.3 %pad_maximum_fusion = bf16[1024,6144]{1,0:T(8,128)(2,1)} fusion(bf16[1024,2048]{1,0:T(8,128)(2,1)S(1)} %convolution_convert_fusion, bf16[1024,2048]{1,0:T(8,128)(2,1)S(1)} %convolution_convert_fusion.1, bf16[1024,2048]{1,0:T(8,128)(2,1)S(1)} %convolution_convert_fusion.2), kind=kLoop, calls=%fused_computation | loop fusion | flops 37748736 | bytes 25165824 | tf_op jit(solution)/shard_map/concatenate | solution.py:72
  234.0 122.2 %reduce-scatter.2.cloned.1.call-done = bf16[64,6144]{1,0:T(8,128)(2,1)} async-done(((bf16[1024,6144]{1,0:T(8,128)(2,1)}), bf16[64,6144]{1,0:T(8,128)(2,1)}) %reduce-scatter.2.cloned.1.call-update) | async-done | bytes 786448 | tf_op jit(solution)/shard_map/reduce_scatter | solution.py:71
  357.9 6.1 stack.2
  364.0 145.9 %all_to_all.104 = bf16[16,64,6144]{2,1,0:T(8,128)(2,1)S(1)} all-to-all(bf16[16,64,6144]{2,1,0:T(8,128)(2,1)} %stack.2), channel_id=1, replica_groups=mesh['expert'=8,'dp'=16] {'dp'}, dimensions={0} | all-to-all | bytes 25165824 | tf_op jit(solution)/shard_map/all_to_all | solution.py:86
  516.8 3.9 copy.90
  520.7 8.3 %reduce.4 = bf16[1024,448]{1,0:T(8,128)(2,1)S(1)} reduce(bf16[1024,1,448]{2,1,0:T(2,128)(2,1)} %bitcast.104, bf16[]{:T(256)} %broadcast.47), dimensions={1}, to_apply=%bitcast.75.reduce_sub_computation | reduce | bytes 1835010
  531.1 4.8 all-to-all-start.5
  535.9 5.8 fusion.16
  541.7 10.1 %all-to-all-done.5 = bf16[16,2,14336]{2,1,0:T(2,128)(2,1)S(1)} async-done(((bf16[16,2,14336]{2,1,0:T(2,128)(2,1)}), bf16[16,2,14336]{2,1,0:T(2,128)(2,1)S(1)}, u32[]{:S(2)}, u32[]{:S(2)}) %all-to-all-start.5) | async-done | bytes 917536 | tf_op jit(solution)/shard_map/all_to_all | solution.py:102
  551.9 3.7 reshape.87
  559.1 11.1 %reshape.80 = bf16[1,64,7168]{1,0,2:T(2,128)(2,1)} reshape(bf16[1,64,16,448]{1,3,2,0:T(8,128)(2,1)} %copy.98) | data formatting | bytes 1835008 | tf_op jit(solution)/shard_map/all_to_all | solution.py:102
  570.3 41.0 %reduce.5 = bf16[7168,64]{1,0:T(8,128)(2,1)} reduce(bf16[7168,1,64]{2,1,0:T(2,128)(2,1)} %bitcast.94, bf16[]{:T(256)} %broadcast.47), dimensions={1}, to_apply=%bitcast.77.reduce_sub_computation | reduce | bytes 1835010
  611.3 4.3 reshape.88
  615.6 4.7 all-to-all-start.6
  620.3 5.9 fusion.19
  626.2 5.5 fusion.22
  634.7 4.1 reshape.89
  638.8 7.2 %copy.93 = bf16[1,64,7168]{2,1,0:T(8,128)(2,1)S(1)} copy(bf16[1,64,7168]{1,0,2:T(2,128)(2,1)} %bitcast.98) | data formatting | bytes 1835008 | tf_op jit(solution)/shard_map/all_to_all | solution.py:101
  (68 shorter events, 49.7 us)
Async XLA Ops:
  7.2 207.4 %copy-start = (bf16[1,448,2048]{2,1,0:T(8,128)(2,1)S(1)}, bf16[1,448,2048]{2,1,0:T(8,128)(2,1)}, u32[]{:S(2)}) copy-start(bf16[1,448,2048]{2,1,0:T(8,128)(2,1)} %param.12) | copy-start | bytes 5505028
  7.2 11.8 %copy-start.6 = (bf16[128,896]{1,0:T(8,128)(2,1)S(1)}, bf16[128,896]{1,0:T(8,128)(2,1)}, u32[]{:S(2)}) copy-start(bf16[128,896]{1,0:T(8,128)(2,1)} %param.7) | copy-start | bytes 688132
  12.6 20.8 %all-to-all-start.2 = ((bf16[8,64,896]{2,1,0:T(8,128)(2,1)}), bf16[8,64,896]{2,1,0:T(8,128)(2,1)S(1)}, u32[]{:S(2)}, u32[]{:S(2)}) async-start(bf16[8,64,896]{2,1,0:T(8,128)(2,1)} %bitcast.12), calls=%async_computation.2 | async-start | bytes 1835008 | tf_op jit(solution)/shard_map/all_to_all | solution.py:53
  33.4 0.9 copy-start.2
  34.3 63.0 %all-to-all-start = ((bf16[8,64,896]{2,1,0:T(8,128)(2,1)}), bf16[8,64,896]{2,1,0:T(8,128)(2,1)S(1)}, u32[]{:S(2)}, u32[]{:S(2)}) async-start(bf16[8,64,896]{2,1,0:T(8,128)(2,1)} %bitcast.5), calls=%async_computation | async-start | bytes 1835008 | tf_op jit(solution)/shard_map/all_to_all | solution.py:46
  97.3 66.6 %all-to-all-start.3 = ((bf16[16,2,14336]{2,1,0:T(2,128)(2,1)}), bf16[16,2,14336]{2,1,0:T(2,128)(2,1)}, u32[]{:S(2)}, u32[]{:S(2)}) async-start(bf16[16,2,14336]{2,1,0:T(2,128)(2,1)} %reshape.82), calls=%async_computation.3 | async-start | bytes 1835008 | tf_op jit(solution)/shard_map/all_to_all | solution.py:52
  163.9 29.7 %all-to-all-start.1 = ((bf16[16,2,14336]{2,1,0:T(2,128)(2,1)}), bf16[16,2,14336]{2,1,0:T(2,128)(2,1)}, u32[]{:S(2)}, u32[]{:S(2)}) async-start(bf16[16,2,14336]{2,1,0:T(2,128)(2,1)} %reshape.84), calls=%async_computation.1 | async-start | bytes 1835008 | tf_op jit(solution)/shard_map/all_to_all | solution.py:45
  171.2 185.0 %reduce-scatter.2.cloned.1.call-start = ((), (), s32[]{:S(2)}) async-start(), calls=%async_computation.8 | async-start | bytes 13369344 | tf_op jit(solution)/shard_map/reduce_scatter | solution.py:71
  214.6 2.4 copy-start.5
  214.6 2.4 copy-start.8
  217.0 2.4 copy-start.3
  217.0 2.4 copy-start.7
  233.0 0.7 copy-start.10
  509.9 4.8 copy-start.1
  509.9 4.8 copy-start.9
  531.1 20.8 %all-to-all-start.5 = ((bf16[16,2,14336]{2,1,0:T(2,128)(2,1)}), bf16[16,2,14336]{2,1,0:T(2,128)(2,1)S(1)}, u32[]{:S(2)}, u32[]{:S(2)}) async-start(bf16[16,2,14336]{2,1,0:T(2,128)(2,1)} %reshape.86), calls=%async_computation.6 | async-start | bytes 1835008 | tf_op jit(solution)/shard_map/all_to_all | solution.py:102
  615.6 19.1 %all-to-all-start.6 = ((bf16[8,2,28672]{2,1,0:T(2,128)(2,1)}), bf16[8,2,28672]{2,1,0:T(2,128)(2,1)S(1)}, u32[]{:S(2)}, u32[]{:S(2)}) async-start(bf16[8,2,28672]{2,1,0:T(2,128)(2,1)} %reshape.88), calls=%async_computation.7 | async-start | bytes 1835008 | tf_op jit(solution)/shard_map/all_to_all | solution.py:101
  620.3 5.9 copy-start.4
Sparse Core Ops, SparseCore 0:
  233.1 123.0 reduce-scatter.1
